TPU v7x, 256 devices: a whole 4x4x8 slice. The times are simulated.
256 devices in a mesh: island: 16 (over z_hi, x, core), fsdp: 16 (over z_lo, y).
Axes of the slice: x: 4, y: 4, z: 8 (z_hi: 2, z_lo: 4; z = z_hi * 4 + z_lo), core: 2. Of those that a mesh axis runs over, the one named last changes fastest.
Arguments:
- tokens: bfloat16 [16, 2048, 3072], P('island', 'fsdp'), may hold values from -6 to 6
- routing: int32 [16, 2048, 2], P('island', 'fsdp'), may hold values from 0 to 7, as said below
- router_weight: bfloat16 [16, 2048, 2], P('island', 'fsdp'), may hold values from 0.19921875 to 1
- w_up: bfloat16 [16, 3072, 8192], P('island', None, 'fsdp'), may hold values from -5 to 5
- w_down: bfloat16 [16, 8192, 3072], P('island', 'fsdp'), may hold values from -5 to 5
- step_number: int32 [1], replicated, may hold values from 0 to 3999
Outputs:
- new_up: bfloat16 [16, 3072, 8192], P('island', None, 'fsdp')
- new_down: bfloat16 [16, 8192, 3072], P('island', 'fsdp')
Inputs may be any that keep to these rules, and one draw needn't show every extreme that they name: `routing`: each row names 2 different experts. In each aligned block of 128 rows (the rows of one device) at most 40 rows name expert 0, at least 20 do, and some block has exactly 40.
All inputs are finite; a program needn't handle non-finite values.
Results may differ from a plain program's by a relative error of at most 0.006.
Values may be sent and summed in bfloat16 or wider, within the bound.
A program may use at most 128 MiB of HBM per device.

v0:
```python
from functools import partial

import jax
import jax.numpy as jnp
from jax import lax
from jax.sharding import PartitionSpec as P

CAP = 40


learn_rate = 4.0


def as_sent(x):
    return jax.tree.map(lambda a: a.astype(jnp.bfloat16) if a.dtype == jnp.float32 else a, x)


def from_partner(value, axis, apart):
    mask = 2**apart
    pairs = [(source, source ^ mask) for source in range(lax.axis_size(axis))]
    return lax.ppermute(value, axis, pairs)


def silu_slope(values):
    sig = jax.nn.sigmoid(values)
    return sig * (1.0 + values * (1.0 - sig))


def dispatch(block_rows, block_routes, block_weight, slot_count):
    is_target = block_routes == 0
    chosen = jnp.any(is_target, axis=1)
    route_share = jnp.sum(
        jnp.where(is_target, block_weight.astype(jnp.float32), jnp.float32(0.0)), axis=1
    )
    slot_index = jnp.cumsum(chosen.astype(jnp.int32)) - 1
    slot_table = (slot_index[None, :] == jnp.arange(slot_count, dtype=jnp.int32)[:, None]) & chosen[
        None, :
    ]
    slot_rows = jnp.dot(
        slot_table.astype(jnp.bfloat16), block_rows, preferred_element_type=jnp.float32
    ).astype(jnp.bfloat16)
    slot_share = jnp.dot(
        slot_table.astype(jnp.float32), route_share, precision=lax.Precision.HIGHEST
    )
    return (slot_rows, slot_share)


def loss_grad(expert_out, slot_rows, slot_share):
    share_col = slot_share[:, None]
    return (share_col * (share_col * expert_out - slot_rows.astype(jnp.float32))).astype(
        jnp.bfloat16
    )


def swap_pair_at(bit_level, stacked):
    return jax.tree.map(
        lambda part, own: part.astype(own.dtype),
        from_partner(as_sent(stacked), "island", bit_level),
        stacked,
    )


def across_bits(helper, operand, bit_index):
    level_count = lax.axis_size("island").bit_length() - 1
    branches = [partial(helper, bit_level) for bit_level in range(level_count)]
    return lax.switch(bit_index, branches, operand)


def on_device(tokens, routing, router_weight, w_up, w_down, step_number):
    own_tokens = tokens[0]
    own_routes = routing[0]
    own_weight = router_weight[0]
    up_cols = w_up[0]
    down_part = w_down[0]
    model_width = own_tokens.shape[1]
    hidden_total = down_part.shape[0] * lax.axis_size("fsdp")
    scale_up = model_width ** (-0.5)
    scale_down = hidden_total ** (-0.5)
    slot_rows, slot_share = dispatch(own_tokens, own_routes, own_weight, CAP)
    gathered = lax.all_gather(slot_rows, "fsdp", axis=0, tiled=True)
    pre_act = scale_up * jnp.dot(gathered, up_cols, preferred_element_type=jnp.float32)
    hidden = jax.nn.silu(pre_act).astype(jnp.bfloat16)
    own_out = lax.psum_scatter(
        scale_down * jnp.dot(hidden, down_part, preferred_element_type=jnp.float32),
        "fsdp",
        scatter_dimension=0,
        tiled=True,
    )
    own_errors = loss_grad(own_out, slot_rows, slot_share)
    errors = lax.all_gather(own_errors, "fsdp", axis=0, tiled=True)
    level_total = lax.axis_size("island").bit_length() - 1
    bit_index = jnp.remainder(step_number[0], jnp.int32(level_total))
    grad_down = scale_down * lax.dot_general(
        hidden, errors, (((0,), (0,)), ((), ())), preferred_element_type=jnp.float32
    )
    moved_down = (down_part.astype(jnp.float32) - learn_rate * grad_down).astype(jnp.bfloat16)
    grad_hidden = scale_down * lax.dot_general(
        errors, down_part, (((1,), (1,)), ((), ())), preferred_element_type=jnp.float32
    )
    grad_pre = (grad_hidden * silu_slope(pre_act)).astype(jnp.bfloat16)
    grad_up = scale_up * lax.dot_general(
        gathered, grad_pre, (((0,), (0,)), ((), ())), preferred_element_type=jnp.float32
    )
    moved_up = (up_cols.astype(jnp.float32) - learn_rate * grad_up).astype(jnp.bfloat16)
    stacked = jnp.stack([moved_up, moved_down.reshape(moved_up.shape)])
    other_pair = across_bits(swap_pair_at, stacked, bit_index)
    other_up = other_pair[0]
    other_down = other_pair[1].reshape(moved_down.shape)
    new_up = (0.5 * (moved_up.astype(jnp.float32) + other_up.astype(jnp.float32))).astype(
        jnp.bfloat16
    )
    new_down = (0.5 * (moved_down.astype(jnp.float32) + other_down.astype(jnp.float32))).astype(
        jnp.bfloat16
    )
    return (new_up[None], new_down[None])


def solution(mesh):
    placed = (
        P("island", "fsdp", None),
        P("island", "fsdp", None),
        P("island", "fsdp", None),
        P("island", None, "fsdp"),
        P("island", "fsdp", None),
        P(),
    )
    return jax.shard_map(
        on_device,
        mesh=mesh,
        in_specs=placed,
        out_specs=(P("island", None, "fsdp"), P("island", "fsdp", None)),
        check_vma=False,
    )
```

profile of v0, /device:TPU:2, one launch (start us, length us, event | category | flops | bytes accessed | tf_op | source)
XLA Modules:
  0.0 490.7 jit_solution(5527915070176468365)
XLA Ops:
  7.2 0.8 fusion.30
  8.0 0.1 copy.9
  8.1 0.2 reduce-window.8
  8.3 0.1 add_reduce_fusion
  8.4 0.9 convolution_convert_fusion
  9.4 91.3 %all-gather.3.cloned.1.call-done = bf16[640,3072]{1,0:T(8,128)(2,1)} async-done(((bf16[40,3072]{1,0:T(8,128)(2,1)}), bf16[640,3072]{1,0:T(8,128)(2,1)}) %all-gather.3.cloned.1.call-update) | async-done | bytes 3932176 | tf_op jit(solution)/shard_map/all_gather | solution.py:80
  100.7 5.4 %fusion.9 = f32[640,512]{1,0:T(8,128)S(1)} fusion(bf16[640,3072]{1,0:T(8,128)(2,1)} %all-gather.3.cloned.1.call-done, bf16[1,3072,512]{2,1,0:T(8,128)(2,1)} %param.13), kind=kOutput, calls=%fused_computation.18 | convolution fusion | flops 2013593600 | bytes 8388608 | tf_op jit(solution)/shard_map/dot_general | solution.py:81
  106.1 5.3 %convolution_multiply_fusion = f32[640,3072]{1,0:T(8,128)} fusion(bf16[1,512,3072]{2,1,0:T(8,128)(2,1)S(1)} %copy-done.4, f32[640,512]{1,0:T(8,128)S(1)} %fusion.9), kind=kOutput, calls=%fused_computation.7 | convolution fusion | flops 2016870400 | bytes 12320768 | tf_op jit(solution)/shard_map/dot_general | solution.py:84
  111.5 0.6 copy-done.2
  112.2 0.1 convolution_bitcast_fusion
  112.3 102.7 %reduce-scatter.2.cloned.1.call-done = f32[40,3072]{1,0:T(8,128)} async-done(((f32[640,3072]{1,0:T(8,128)}), f32[40,3072]{1,0:T(8,128)}) %reduce-scatter.2.cloned.1.call-update) | async-done | bytes 491536 | tf_op jit(solution)/shard_map/reduce_scatter | solution.py:83
  215.0 1.9 multiply_convert_fusion.2
  217.6 84.1 %all-gather.5.cloned.1.call-done = bf16[640,3072]{1,0:T(8,128)(2,1)} async-done(((bf16[40,3072]{1,0:T(8,128)(2,1)}), bf16[640,3072]{1,0:T(8,128)(2,1)}) %all-gather.5.cloned.1.call-update) | async-done | bytes 3932176 | tf_op jit(solution)/shard_map/all_gather | solution.py:90
  301.6 6.8 %subtract_convert_fusion = bf16[512,3072]{1,0:T(8,128)(2,1)} fusion(bf16[640,3072]{1,0:T(8,128)(2,1)} %all-gather.5.cloned.1.call-done, bf16[1,512,3072]{2,1,0:T(8,128)(2,1)} %param.14, f32[640,512]{1,0:T(8,128)S(1)} %fusion.9), kind=kOutput, calls=%fused_computation.5 | convolution fusion | flops 2021195776 | bytes 11534336 | tf_op jit(solution)/shard_map/dot_general | solution.py:93
  308.5 6.3 %stack_reshape.3 = bf16[1,3072,512]{2,1,0:T(8,128)(2,1)} reshape(bf16[512,3072]{1,0:T(8,128)(2,1)} %subtract_convert_fusion) | data formatting | bytes 6291456 | tf_op jit(solution)/shard_map/stack;reshape | solution.py:105
  314.8 11.9 %subtract_convert_fusion.1 = bf16[3072,512]{1,0:T(8,128)(2,1)} fusion(bf16[640,3072]{1,0:T(8,128)(2,1)} %all-gather.3.cloned.1.call-done, bf16[1,3072,512]{2,1,0:T(8,128)(2,1)} %param.13, bf16[640,3072]{1,0:T(8,128)(2,1)} %all-gather.5.cloned.1.call-done, bf16[1,512,3072]{2,1,0:T(8,128)(2,1)} %param.14, f32[640,512]{1,0:T(8,128)S(1)} %fusion.9), kind=kOutput, calls=%fused_computation.6 | convolution fusion | flops 4036100096 | bytes 18612224 | tf_op jit(solution)/shard_map/dot_general | solution.py:101
  326.6 3.4 pad_maximum_fusion
  330.0 128.6 %conditional.1 = (bf16[2,3072,512]{2,1,0:T(8,128)(2,1)}) conditional(s32[]{:T(128)} %clamp.3, bf16[2,3072,512]{2,1,0:T(8,128)(2,1)S(1)} %pad_maximum_fusion, bf16[2,3072,512]{2,1,0:T(8,128)(2,1)S(1)} %pad_maximum_fusion, bf16[2,3072,512]{2,1,0:T(8,128)(2,1)S(1)} %pad_maximum_fusion, ...), branch_computations={%region_4.5_spmd, %region_5.6_spmd, %region_6.7_spmd, %region_7.8_... | conditional | bytes 25165872 | solution.py:66
  330.1 0.6 collective-permute-start.1
  330.7 127.9 %collective-permute-done.1 = bf16[2,3072,512]{2,1,0:T(8,128)(2,1)} collective-permute-done((bf16[2,3072,512]{2,1,0:T(8,128)(2,1)S(1)}, bf16[2,3072,512]{2,1,0:T(8,128)(2,1)}, u32[]{:S(2)}, u32[]{:S(2)}) %collective-permute-start.1) | collective-permute-done | bytes 6291488 | tf_op jit(solution)/shard_map/cond/branch_1_fun/ppermute | solution.py:21
  458.6 5.5 %fusion.3 = bf16[1,3072,512]{2,1,0:T(8,128)(2,1)} fusion(bf16[3072,512]{1,0:T(8,128)(2,1)} %subtract_convert_fusion.1, bf16[2,3072,512]{2,1,0:T(8,128)(2,1)} %get-tuple-element.11), kind=kLoop, calls=%fused_computation.10 | loop fusion | flops 7864320 | bytes 9437184 | tf_op jit(solution)/shard_map/broadcast_in_dim | solution.py:115
  464.1 5.4 %slice_convert_fusion = f32[1,3072,512]{2,1,0:T(8,128)} fusion(bf16[2,3072,512]{2,1,0:T(8,128)(2,1)} %get-tuple-element.11), kind=kLoop, calls=%fused_computation.11 | loop fusion | flops 1572864 | bytes 9437184 | tf_op jit(solution)/shard_map/convert_element_type | solution.py:112
  469.6 8.1 %reshape.49 = f32[512,3072]{1,0:T(8,128)} reshape(f32[1,3072,512]{2,1,0:T(8,128)} %slice_convert_fusion) | data formatting | bytes 12582912 | tf_op jit(solution)/shard_map/convert_element_type | solution.py:112
  477.7 6.4 %fusion.2 = bf16[1,512,3072]{2,1,0:T(8,128)(2,1)} fusion(f32[512,3072]{1,0:T(8,128)} %reshape.49, bf16[512,3072]{1,0:T(8,128)(2,1)} %subtract_convert_fusion), kind=kLoop, calls=%fused_computation.9 | loop fusion | flops 6291456 | bytes 12582912 | tf_op jit(solution)/shard_map/broadcast_in_dim | solution.py:115
  (17 shorter events, 0.2 us)
Async XLA Ops:
  7.2 1.2 copy-start
  7.2 93.5 %all-gather.3.cloned.1.call-start = ((), (), s32[]{:S(2)}) async-start(), calls=%async_computation.1 | async-start | bytes 4177920 | tf_op jit(solution)/shard_map/all_gather | solution.py:80
  9.4 205.7 %reduce-scatter.2.cloned.1.call-start = ((), (), s32[]{:S(2)}) async-start(), calls=%async_computation.2 | async-start | bytes 8355840 | tf_op jit(solution)/shard_map/reduce_scatter | solution.py:83
  100.7 5.4 %copy-start.4 = (bf16[1,512,3072]{2,1,0:T(8,128)(2,1)S(1)}, bf16[1,512,3072]{2,1,0:T(8,128)(2,1)}, u32[]{:S(2)}) copy-start(bf16[1,512,3072]{2,1,0:T(8,128)(2,1)} %param.14) | copy-start | bytes 9437188
  111.5 0.7 copy-start.2
  111.5 0.7 copy-start.3
  111.5 103.5 %copy-start.1 = (bf16[40,3072]{1,0:T(8,128)(2,1)S(1)}, bf16[40,3072]{1,0:T(8,128)(2,1)}, u32[]{:S(2)}) copy-start(bf16[40,3072]{1,0:T(8,128)(2,1)} %convolution_convert_fusion) | copy-start | bytes 737284
  111.5 190.2 %all-gather.5.cloned.1.call-start = ((), (), s32[]{:S(2)}) async-start(), calls=%async_computation.3 | async-start | bytes 4177920 | tf_op jit(solution)/shard_map/all_gather | solution.py:90
  330.1 128.6 %collective-permute-start.1 = (bf16[2,3072,512]{2,1,0:T(8,128)(2,1)S(1)}, bf16[2,3072,512]{2,1,0:T(8,128)(2,1)}, u32[]{:S(2)}, u32[]{:S(2)}) collective-permute-start(bf16[2,3072,512]{2,1,0:T(8,128)(2,1)S(1)} %param.1), channel_id=1, source_target_pairs={{0,32},{16,48},{32,0},{48,16},{64,96},{80,112},{96,64},{112,80},{1... | collective-permute-start | bytes 18874376 | tf_op jit(solution)/shard_map/cond/branch_1_fun/ppermute | solution.py:21
Sparse Core Ops, SparseCore 0:
  10.4 90.2 all-gather.2
  111.6 103.3 reduce-scatter.1
  217.4 84.2 all-gather.4
where the time goes:
time: 491 us
  waiting for transfers between devices  406 us (83%)
  matrix products  30.5 us (6%)
  other arithmetic  23.7 us (5%)
  local copies, waits for them, and re-layouts  15.1 us (3%)
  between operations  14.5 us (3%)
    ppermute x1, waiting for transfers between devices, from_partner(): return lax.ppermute(value, axis, pairs)  128 us
    reduce_scatter x1, waiting for transfers between devices, on_device(): lax.psum_scatter(scale_down * jnp.dot(hidden, down_part, preferred_elemen...  103 us
    all_gather x1, waiting for transfers between devices, on_device(): gathered = lax.all_gather(slot_rows, 'fsdp', axis=0, tiled=True)  91.3 us
    all_gather x1, waiting for transfers between devices, on_device(): errors = lax.all_gather(own_errors, 'fsdp', axis=0, tiled=True)  84.1 us
    broadcast_in_dim x2, other arithmetic, on_device(): return (new_up[None], new_down[None])  11.9 us
    dot_general x1, matrix products, on_device(): lax.dot_general(gathered, grad_pre, (((0,), (0,)), ((), ())), preferred_e...  11.9 us
  transfers between devices with their start and end apart: 4, of which 4 were waited for; matrix products, arithmetic and copies ran while one was open for 0% of the time, Pallas kernels for 0%

commit v1 on v0

v1 whole, which is shorter than its diff:
```python
from functools import partial

import jax
import jax.numpy as jnp
from jax import lax
from jax.experimental import pallas as pl
from jax.experimental.pallas import tpu as pltpu
from jax.sharding import PartitionSpec as P

MESH = pl.DeviceIdType.MESH
F32, BF16 = jnp.float32, jnp.bfloat16
CAP = 40
PAIR = 2 * CAP
STAGE = 48
SIDE = 4
GROUP = SIDE * PAIR
LANES = 128

learn_rate = 4.0


def silu_slope(values):
    sig = jax.nn.sigmoid(values)
    return sig * (1.0 + values * (1.0 - sig))


def unit(ref, yy, zz, low=0, size=None):
    start = pl.multiple_of(((yy // 2) * SIDE + zz) * PAIR, 16)
    size = ref.shape[-1] if size is None else size
    return ref.at[yy % 2, pl.ds(start, PAIR), pl.ds(low, size)]


def place():
    me = lax.axis_index("fsdp")
    return me // SIDE, me % SIDE


def across(z, k):
    return (z, z + 1 - 2 * (z % 2), (z + 2) % SIDE, SIDE - 1 - z)[k]


class Sender:
    def __init__(self):
        self.started = []

    def send(self, src, dst, send_sem, recv_sem, device):
        copy = pltpu.make_async_remote_copy(
            src_ref=src,
            dst_ref=dst,
            send_sem=send_sem,
            recv_sem=recv_sem,
            device_id=device,
            device_id_type=MESH,
        )
        copy.start()
        self.started.append(copy)

    def drain(self):
        for copy in self.started:
            copy.wait_send()
        self.started = []


def arrived(dst, sems, recv_sem, device):
    pltpu.make_async_remote_copy(
        src_ref=dst, dst_ref=dst, send_sem=sems, recv_sem=recv_sem, device_id=device, device_id_type=MESH
    ).wait_recv()


def at(zz, yy):
    return {"fsdp": zz * SIDE + yy}


class Gather:
    def __init__(self, buf, send_sem, full_sem, half_sem, out):
        self.buf, self.send_sem, self.full_sem, self.half_sem, self.out = buf, send_sem, full_sem, half_sem, out
        self.z, self.y = place()
        self.part = buf.shape[-1] // 2

    def wait_full(self, yy, zz):
        view = unit(self.buf, yy, zz)
        arrived(view, self.send_sem.at[0], self.full_sem.at[yy * SIDE + zz], at(self.z, (self.y + 1) % SIDE))

    def push(self, k):
        z, y = self.z, self.y
        zz = across(z, k)
        if k > 0:
            self.wait_full(y, zz)
        view = unit(self.buf, y, zz)
        for i, step in enumerate((1, SIDE - 1)):
            self.out.send(
                view, view, self.send_sem.at[3 + 2 * k + i], self.full_sem.at[y * SIDE + zz], at(z, (y + step) % SIDE)
            )

    def forward(self, k):
        z, y = self.z, self.y
        zz = across(z, k)
        for i, step in enumerate((1, SIDE - 1)):
            source = (y + SIDE - step) % SIDE
            self.wait_full(source, zz)
            view = unit(self.buf, source, zz, i * self.part, self.part)
            self.out.send(
                view,
                view,
                self.send_sem.at[11 + 2 * k + i],
                self.half_sem.at[i, source * SIDE + zz],
                at(z, (y + step) % SIDE),
            )

    def run(self):
        z, y = self.z, self.y
        own = unit(self.buf, y, z)
        for k in (3, 2, 1):
            self.out.send(own, own, self.send_sem.at[k - 1], self.full_sem.at[y * SIDE + z], at(across(z, k), y))
        for k in range(SIDE):
            self.push(k)
            if k > 0:
                self.forward(k - 1)
        self.forward(SIDE - 1)

    def finish(self):
        z, y = self.z, self.y
        far = (y + 2) % SIDE
        for k in range(SIDE):
            zz = across(z, k)
            for i in range(2):
                view = unit(self.buf, far, zz, i * self.part, self.part)
                arrived(view, self.send_sem.at[0], self.half_sem.at[i, far * SIDE + zz], at(z, (y + 1) % SIDE))


def expert_kernel(
    scale_up,
    scale_down,
    tokens,
    routes,
    weights,
    up_hbm,
    down_hbm,
    slots_out,
    errors_out,
    pre_out,
    slots,
    errors,
    up,
    down,
    pre,
    hidden,
    part,
    got_half,
    got_full,
    got_z,
    total,
    stage_out,
    stage_in,
    share_col,
    load_sem,
    store_sem,
    stage_sem,
    gather_send,
    gather_full,
    gather_half,
    sum_send,
    sum_half,
    sum_full,
    sum_z,
):
    z, y = place()
    half = tokens.shape[1] // 2
    quarter = half // 2
    out = Sender()
    y_up, y_down, y_far = (y + 1) % SIDE, (y + SIDE - 1) % SIDE, (y + 2) % SIDE
    y_pair = y + 1 - 2 * (y % 2)

    loads = [
        pltpu.make_async_copy(up_hbm, up, load_sem.at[0]),
        pltpu.make_async_copy(down_hbm, down, load_sem.at[1]),
    ]
    for load in loads:
        load.start()
    barrier = pltpu.get_barrier_semaphore()
    peers = [at(across(z, k), y) for k in (1, 2, 3)] + [at(z, y_up), at(z, y_down)]
    for peer in peers:
        pl.semaphore_signal(barrier, inc=1, device_id=peer, device_id_type=MESH)

    target0 = routes[0:1, :] == 0
    target1 = routes[1:2, :] == 0
    chosen = (target0 | target1).astype(F32)
    share_row = jnp.where(target0, weights[0:1, :], 0.0) + jnp.where(target1, weights[1:2, :], 0.0)
    count = chosen.shape[1]
    earlier = lax.broadcasted_iota(jnp.int32, (count, count), 0) <= lax.broadcasted_iota(jnp.int32, (count, count), 1)
    ranks = jnp.dot(
        jnp.broadcast_to(chosen, (8, count)).astype(BF16), earlier.astype(BF16), preferred_element_type=F32
    )[0:1, :]
    slot_ids = lax.broadcasted_iota(jnp.int32, (STAGE, count), 0).astype(F32)
    takes = (slot_ids == ranks - 1.0) & (chosen > 0.0) & (slot_ids < float(CAP))
    table = jnp.where(takes, 1.0, 0.0).astype(BF16)
    own_share = jnp.sum(jnp.where(takes, share_row, 0.0), axis=1, keepdims=True)
    mine = y % 2
    own_rows = jnp.dot(
        table, tokens[:, pl.ds(pl.multiple_of(mine * half, LANES), half)], preferred_element_type=F32
    )
    stage_out[:, 0:half] = jnp.dot(
        table, tokens[:, pl.ds(pl.multiple_of((1 - mine) * half, LANES), half)], preferred_element_type=F32
    ).astype(BF16)
    stage_out[:, half:] = jnp.broadcast_to(own_share, (STAGE, LANES)).astype(BF16)
    pl.semaphore_wait(barrier, len(peers))
    out.send(stage_out, stage_in, stage_sem.at[0], stage_sem.at[1], at(z, y_pair))
    arrived(stage_in, stage_sem.at[0], stage_sem.at[1], at(z, y_pair))
    other_rows = stage_in[:, 0:half].astype(F32)
    other_share = stage_in[:, half:].astype(F32)[0:CAP, 0:1]
    first = mine == 0
    own_rows, own_share, other_rows = own_rows[0:CAP], own_share[0:CAP], other_rows[0:CAP]
    rows = jnp.concatenate(
        [jnp.where(first, own_rows, other_rows), jnp.where(first, other_rows, own_rows)], axis=0
    ).astype(BF16)
    unit(slots, y, z)[...] = rows
    share_col[...] = jnp.broadcast_to(
        jnp.concatenate(
            [jnp.where(first, own_share, other_share), jnp.where(first, other_share, own_share)], axis=0
        ),
        (PAIR, LANES),
    )

    spread = Gather(slots, gather_send.at[0], gather_full.at[0], gather_half.at[0], out)
    spread.run()

    def ahead(group):
        begin = pl.multiple_of(group * GROUP, 16)
        block = pl.ds(begin, GROUP)
        values = scale_up * (
            jnp.dot(slots[0, block, :], up[0:half, :], preferred_element_type=F32)
            + jnp.dot(slots[1, block, :], up[half:, :], preferred_element_type=F32)
        )
        pre[block, :] = values
        hidden[block, :] = jax.nn.silu(values).astype(BF16)

    for load in loads:
        load.wait()
    ahead(y // 2)
    spread.finish()
    ahead(1 - y // 2)
    stores = [
        pltpu.make_async_copy(slots.at[0], slots_out.at[:, 0:half], store_sem.at[0]),
        pltpu.make_async_copy(slots.at[1], slots_out.at[:, half : 2 * half], store_sem.at[1]),
        pltpu.make_async_copy(pre, pre_out, store_sem.at[2]),
    ]
    for store in stores:
        store.start()

    def column(yy):
        begin = pl.multiple_of((yy // 2) * GROUP, 16)
        block = pl.ds(begin, GROUP)
        side = yy % 2
        width = half // 3
        for j in range(3):
            part[side, block, j * width : (j + 1) * width] = (
                scale_down
                * jnp.dot(
                    hidden[block, :],
                    down[:, pl.ds(pl.multiple_of(side * half + j * width, LANES), width)],
                    preferred_element_type=F32,
                )
            ).astype(BF16)

    column(y_far)
    for zz in range(SIDE):
        for i, target in enumerate((y_down, y_up)):
            out.send(
                unit(part, y_far, zz, i * quarter, quarter),
                got_half.at[i, zz],
                sum_send.at[2 * zz + i],
                sum_half.at[i, zz],
                at(z, target),
            )
    column(y_down)
    column(y_up)
    for zz in range(SIDE):
        for i, target in enumerate((y_down, y_up)):
            arrived(got_half.at[i, zz], sum_send.at[0], sum_half.at[i, zz], at(z, target))
            view = unit(part, target, zz, i * quarter, quarter)
            view[...] = (view[...].astype(F32) + got_half[i, zz].astype(F32)).astype(BF16)
            out.send(
                unit(part, target, zz),
                got_full.at[i, zz],
                sum_send.at[8 + 2 * zz + i],
                sum_full.at[i, zz],
                at(z, target),
            )
    column(y)
    for k in (3, 2, 1, 0):
        zz = across(z, k)
        for i in range(2):
            arrived(got_full.at[i, zz], sum_send.at[0], sum_full.at[i, zz], at(z, y_up))
        view = unit(part, y, zz)
        added = view[...].astype(F32) + got_full[0, zz].astype(F32) + got_full[1, zz].astype(F32)
        if k == 0:
            total[...] = added
        else:
            view[...] = added.astype(BF16)
            out.send(view, got_z.at[k - 1], sum_send.at[15 + k], sum_z.at[k - 1], at(zz, y))
    for k in (1, 2, 3):
        arrived(got_z.at[k - 1], sum_send.at[0], sum_z.at[k - 1], at(across(z, k), y))
    result = total[...] + got_z[0].astype(F32) + got_z[1].astype(F32) + got_z[2].astype(F32)
    share = share_col[:, 0:1]
    unit(errors, y, z)[...] = (share * (share * result - unit(slots, y, z)[...].astype(F32))).astype(BF16)

    back = Gather(errors, gather_send.at[1], gather_full.at[1], gather_half.at[1], out)
    back.run()
    back.finish()
    last = [
        pltpu.make_async_copy(errors.at[0], errors_out.at[:, 0:half], store_sem.at[3]),
        pltpu.make_async_copy(errors.at[1], errors_out.at[:, half : 2 * half], store_sem.at[4]),
    ]
    for store in last:
        store.start()
    out.drain()
    for store in stores + last:
        store.wait()


def expert(tokens, routes, weights, up, down):
    width = tokens.shape[1]
    units = up.shape[1]
    half = width // 2
    slot_count = SIDE * SIDE * CAP
    hidden_total = units * SIDE * SIDE
    vmem = pl.BlockSpec(memory_space=pltpu.VMEM)
    hbm = pl.BlockSpec(memory_space=pl.ANY)
    dma = pltpu.SemaphoreType.DMA
    return pl.pallas_call(
        partial(expert_kernel, width ** (-0.5), hidden_total ** (-0.5)),
        out_shape=(
            jax.ShapeDtypeStruct((slot_count, width), BF16),
            jax.ShapeDtypeStruct((slot_count, width), BF16),
            jax.ShapeDtypeStruct((slot_count, units), F32),
        ),
        in_specs=[vmem, vmem, vmem, hbm, hbm],
        out_specs=(hbm, hbm, hbm),
        scratch_shapes=[
            pltpu.VMEM((2, slot_count, half), BF16),
            pltpu.VMEM((2, slot_count, half), BF16),
            pltpu.VMEM((width, units), BF16),
            pltpu.VMEM((units, width), BF16),
            pltpu.VMEM((slot_count, units), F32),
            pltpu.VMEM((slot_count, units), BF16),
            pltpu.VMEM((2, slot_count, half), BF16),
            pltpu.VMEM((2, SIDE, PAIR, half // 2), BF16),
            pltpu.VMEM((2, SIDE, PAIR, half), BF16),
            pltpu.VMEM((SIDE - 1, PAIR, half), BF16),
            pltpu.VMEM((PAIR, half), F32),
            pltpu.VMEM((STAGE, half + LANES), BF16),
            pltpu.VMEM((STAGE, half + LANES), BF16),
            pltpu.VMEM((PAIR, LANES), F32),
            dma((2,)),
            dma((5,)),
            dma((2,)),
            dma((2, 19)),
            dma((2, SIDE * SIDE)),
            dma((2, 2, SIDE * SIDE)),
            dma((19,)),
            dma((2, SIDE)),
            dma((2, SIDE)),
            dma((SIDE - 1,)),
        ],
        compiler_params=pltpu.CompilerParams(
            collective_id=0, has_side_effects=True, vmem_limit_bytes=48 * 1024 * 1024
        ),
        cost_estimate=pl.CostEstimate(
            flops=4 * slot_count * width * units, bytes_accessed=200_000_000, transcendentals=slot_count * units
        ),
    )(tokens, routes, weights, up, down)


def on_device(tokens, routing, router_weight, w_up, w_down, step_number):
    up, down = w_up[0], w_down[0]
    width, units = up.shape
    scale_up = width ** (-0.5)
    scale_down = (units * lax.axis_size("fsdp")) ** (-0.5)
    slots, errors, pre_act = expert(
        tokens[0], routing[0].T, router_weight[0].T.astype(F32), up, down
    )
    hidden = jax.nn.silu(pre_act).astype(BF16)
    grad_down = scale_down * lax.dot_general(
        hidden, errors, (((0,), (0,)), ((), ())), preferred_element_type=F32
    )
    moved_down = (down.astype(F32) - learn_rate * grad_down).astype(BF16)
    grad_hidden = scale_down * lax.dot_general(
        errors, down, (((1,), (1,)), ((), ())), preferred_element_type=F32
    )
    grad_pre = (grad_hidden * silu_slope(pre_act)).astype(BF16)
    grad_up = scale_up * lax.dot_general(
        slots, grad_pre, (((0,), (0,)), ((), ())), preferred_element_type=F32
    )
    moved_up = (up.astype(F32) - learn_rate * grad_up).astype(BF16)

    def swap(bit, moved):
        size = lax.axis_size("island")
        pairs = [(source, source ^ (1 << bit)) for source in range(size)]
        other = [lax.ppermute(value, "island", pairs) for value in moved]
        return tuple((0.5 * (a.astype(F32) + b.astype(F32))).astype(BF16) for a, b in zip(moved, other))

    levels = lax.axis_size("island").bit_length() - 1
    bit_index = jnp.remainder(step_number[0], jnp.int32(levels))
    new_up, new_down = lax.switch(
        bit_index, [partial(swap, bit) for bit in range(levels)], (moved_up, moved_down)
    )
    return (new_up[None], new_down[None])


def solution(mesh):
    placed = (
        P("island", "fsdp", None),
        P("island", "fsdp", None),
        P("island", "fsdp", None),
        P("island", None, "fsdp"),
        P("island", "fsdp", None),
        P(),
    )
    return jax.shard_map(
        on_device,
        mesh=mesh,
        in_specs=placed,
        out_specs=(P("island", None, "fsdp"), P("island", "fsdp", None)),
        check_vma=False,
    )
```

time: 491 us -> 313 us (0.64)
  the two profiles are of different devices: /device:TPU:2 before, /device:TPU:228 now
where the time goes in v1:
time: 313 us
  Pallas kernels  149 us (48%)
  waiting for transfers between devices  130 us (42%)
  matrix products  17.8 us (6%)
  other arithmetic  6.22 us (2%)
  local copies, waits for them, and re-layouts  4.76 us (2%)
  starting transfers between devices  3.62 us (1%)
    pallas_call x1, Pallas kernels, expert(): pl.pallas_call(partial(expert_kernel, width ** (-0.5), hidden_total ** (-...  149 us
    ppermute x2, waiting for transfers between devices, swap(): other = [lax.ppermute(value, 'island', pairs) for value in moved]  130 us
    dot_general x1, matrix products, on_device(): lax.dot_general(slots, grad_pre, (((0,), (0,)), ((), ())), preferred_elem...  11.3 us
    dot_general x1, matrix products, on_device(): lax.dot_general(hidden, errors, (((0,), (0,)), ((), ())), preferred_eleme...  6.49 us
  transfers between devices with their start and end apart: 2, of which 2 were waited for; matrix products, arithmetic and copies ran while one was open for 1% of the time, Pallas kernels for 0%

profile of v1, /device:TPU:228, one launch (start us, length us, event | category | flops | bytes accessed | tf_op | source)
XLA Modules:
  0.0 312.7 jit_solution(13273898544928697435)
XLA Ops:
  1.3 0.7 convert_bitcast_fusion.weights
  2.0 0.0 copy-start
  2.0 1.9 copy-done
  3.8 0.0 copy-start.2
  3.8 1.1 copy-done.2
  5.0 0.0 copy-start.3
  5.0 0.7 copy-done.3
  5.7 0.0 copy-start.1
  5.7 149.0 %shard_map.85 = (bf16[640,3072]{1,0:T(8,128)(2,1)}, bf16[640,3072]{1,0:T(8,128)(2,1)}, f32[640,512]{1,0:T(8,128)S(1)}) custom-call(bf16[128,3072]{1,0:T(8,128)(2,1)S(1)} %bitcast.40, s32[2,128]{1,0:T(2,128)S(1)} %bitcast.41, f32[2,128]{1,0:T(2,128)S(1)} %convert_bitcast_fusion.weights, bf16[3072,512]{1,0:T(8,128)(2,1)S(1)} %bitcast.39, ...), custom_call_target="tpu_custom_call" | custom-call | flops 4026531840 | bytes 200000000 | tf_op jit(solution)/shard_map/pallas_call | solution.py:330
  154.6 0.0 copy-start.4
  154.6 1.0 copy-done.4
  155.7 0.0 copy-done.1
  155.7 11.3 %subtract_convert_fusion.1 = bf16[3072,512]{1,0:T(8,128)(2,1)} fusion(bf16[640,3072]{1,0:T(8,128)(2,1)} %get-tuple-element.31, bf16[640,3072]{1,0:T(8,128)(2,1)} %get-tuple-element.32, f32[640,512]{1,0:T(8,128)} %copy-done.4, bf16[1,512,3072]{2,1,0:T(8,128)(2,1)} %param.14, bf16[1,3072,512]{2,1,0:T(8,128)(2,1)S(1)} %copy-done.1), kind=kOutput, calls=%fused_computation.17 | convolution fusion | flops 4036100096 | bytes 18612224 | tf_op jit(solution)/shard_map/dot_general | solution.py:391
  167.0 0.0 copy-start.5
  167.0 6.5 %subtract_convert_fusion = bf16[512,3072]{1,0:T(8,128)(2,1)S(1)} fusion(bf16[640,3072]{1,0:T(8,128)(2,1)} %get-tuple-element.32, f32[640,512]{1,0:T(8,128)} %copy-done.4, bf16[1,512,3072]{2,1,0:T(8,128)(2,1)} %param.14), kind=kOutput, calls=%fused_computation.16 | convolution fusion | flops 2021195776 | bytes 11534336 | tf_op jit(solution)/shard_map/dot_general | solution.py:383
  173.5 0.0 copy-done.5
  173.5 139.2 %conditional.1 = (bf16[1,3072,512]{2,1,0:T(8,128)(2,1)}, bf16[1,512,3072]{2,1,0:T(8,128)(2,1)}) conditional(s32[]{:T(128)} %clamp.3, (bf16[3072,512]{1,0:T(8,128)(2,1)S(1)}, bf16[512,3072]{1,0:T(8,128)(2,1)S(1)}) %tuple.44, (bf16[3072,512]{1,0:T(8,128)(2,1)S(1)}, bf16[512,3072]{1,0:T(8,128)(2,1)S(1)}) %tuple.45, ...), branch_computations={%region_0.1_spmd, %region_1.2_spmd, %region_2.3_spmd, %region_3.4_... | conditional | flops 15728640 | bytes 44040288 | solution.py:404
  173.7 0.6 collective-permute-start.4
  174.3 3.0 collective-permute-start.5
  177.3 69.0 %collective-permute-done.4 = bf16[3072,512]{1,0:T(8,128)(2,1)S(1)} collective-permute-done((bf16[3072,512]{1,0:T(8,128)(2,1)S(1)}, bf16[3072,512]{1,0:T(8,128)(2,1)S(1)}, u32[]{:S(2)}, u32[]{:S(2)}) %collective-permute-start.4) | collective-permute-done | bytes 3145760 | tf_op jit(solution)/shard_map/cond/branch_2_fun/ppermute | solution.py:399
  246.3 2.7 fusion.4
  249.0 60.8 %collective-permute-done.5 = bf16[512,3072]{1,0:T(8,128)(2,1)S(1)} collective-permute-done((bf16[512,3072]{1,0:T(8,128)(2,1)S(1)}, bf16[512,3072]{1,0:T(8,128)(2,1)S(1)}, u32[]{:S(2)}, u32[]{:S(2)}) %collective-permute-start.5) | collective-permute-done | bytes 3145760 | tf_op jit(solution)/shard_map/cond/branch_2_fun/ppermute | solution.py:399
  309.8 2.9 fusion.5
Async XLA Ops:
  2.0 1.9 copy-start
  3.8 1.1 copy-start.2
  5.0 0.7 copy-start.3
  5.7 150.0 %copy-start.1 = (bf16[1,3072,512]{2,1,0:T(8,128)(2,1)S(1)}, bf16[1,3072,512]{2,1,0:T(8,128)(2,1)}, u32[]{:S(2)}) copy-start(bf16[1,3072,512]{2,1,0:T(8,128)(2,1)} %param.13) | copy-start | bytes 9437188
  154.6 1.1 copy-start.4
  167.0 6.5 %copy-start.5 = (bf16[3072,512]{1,0:T(8,128)(2,1)S(1)}, bf16[3072,512]{1,0:T(8,128)(2,1)}, u32[]{:S(2)}) copy-start(bf16[3072,512]{1,0:T(8,128)(2,1)} %subtract_convert_fusion.1) | copy-start | bytes 9437188
  173.7 72.6 %collective-permute-start.4 = (bf16[3072,512]{1,0:T(8,128)(2,1)S(1)}, bf16[3072,512]{1,0:T(8,128)(2,1)S(1)}, u32[]{:S(2)}, u32[]{:S(2)}) collective-permute-start(bf16[3072,512]{1,0:T(8,128)(2,1)S(1)} %get-tuple-element.22), channel_id=1, source_target_pairs={{0,64},{16,80},{32,96},{48,112},{64,0},{80,16},{96,32},{112,48},{1... | collective-permute-start | bytes 9437192 | tf_op jit(solution)/shard_map/cond/branch_2_fun/ppermute | solution.py:399
  174.3 135.5 %collective-permute-start.5 = (bf16[512,3072]{1,0:T(8,128)(2,1)S(1)}, bf16[512,3072]{1,0:T(8,128)(2,1)S(1)}, u32[]{:S(2)}, u32[]{:S(2)}) collective-permute-start(bf16[512,3072]{1,0:T(8,128)(2,1)S(1)} %get-tuple-element.23), channel_id=1, source_target_pairs={{0,64},{16,80},{32,96},{48,112},{64,0},{80,16},{96,32},{112,48},{1... | collective-permute-start | bytes 9437192 | tf_op jit(solution)/shard_map/cond/branch_2_fun/ppermute | solution.py:399

commit v2 on v1

v2 whole, which is shorter than its diff:
```python
from functools import partial

import jax
import jax.numpy as jnp
from jax import lax
from jax.experimental import pallas as pl
from jax.experimental.pallas import tpu as pltpu
from jax.sharding import PartitionSpec as P

MESH = pl.DeviceIdType.MESH
F32, BF16 = jnp.float32, jnp.bfloat16
CAP = 40
PAIR = 2 * CAP
STAGE = 48
SIDE = 4
GROUP = SIDE * PAIR
LANES = 128
TILE = 512
UNIT_TILE = 256

learn_rate = 4.0


def silu_slope(values):
    sig = jax.nn.sigmoid(values)
    return sig * (1.0 + values * (1.0 - sig))


def unit(ref, yy, zz, low=0, size=None):
    start = pl.multiple_of(((yy // 2) * SIDE + zz) * PAIR, 16)
    size = ref.shape[-1] if size is None else size
    return ref.at[yy % 2, pl.ds(start, PAIR), pl.ds(low, size)]


def place():
    me = lax.axis_index("fsdp")
    return me // SIDE, me % SIDE


def across(z, k):
    return (z, z + 1 - 2 * (z % 2), (z + 2) % SIDE, SIDE - 1 - z)[k]


class Sender:
    def __init__(self):
        self.started = []

    def send(self, src, dst, send_sem, recv_sem, device):
        copy = pltpu.make_async_remote_copy(
            src_ref=src,
            dst_ref=dst,
            send_sem=send_sem,
            recv_sem=recv_sem,
            device_id=device,
            device_id_type=MESH,
        )
        copy.start()
        self.started.append(copy)

    def drain(self):
        for copy in self.started:
            copy.wait_send()
        self.started = []


def arrived(dst, sems, recv_sem, device):
    pltpu.make_async_remote_copy(
        src_ref=dst, dst_ref=dst, send_sem=sems, recv_sem=recv_sem, device_id=device, device_id_type=MESH
    ).wait_recv()


def at(zz, yy):
    return {"fsdp": zz * SIDE + yy}


class Gather:
    def __init__(self, buf, send_sem, full_sem, half_sem, out):
        self.buf, self.send_sem, self.full_sem, self.half_sem, self.out = buf, send_sem, full_sem, half_sem, out
        self.z, self.y = place()
        self.part = buf.shape[-1] // 2

    def wait_full(self, yy, zz):
        view = unit(self.buf, yy, zz)
        arrived(view, self.send_sem.at[0], self.full_sem.at[yy * SIDE + zz], at(self.z, (self.y + 1) % SIDE))

    def push(self, k):
        z, y = self.z, self.y
        zz = across(z, k)
        if k > 0:
            self.wait_full(y, zz)
        view = unit(self.buf, y, zz)
        for i, step in enumerate((1, SIDE - 1)):
            self.out.send(
                view, view, self.send_sem.at[3 + 2 * k + i], self.full_sem.at[y * SIDE + zz], at(z, (y + step) % SIDE)
            )

    def forward(self, k):
        z, y = self.z, self.y
        zz = across(z, k)
        for i, step in enumerate((1, SIDE - 1)):
            source = (y + SIDE - step) % SIDE
            self.wait_full(source, zz)
            view = unit(self.buf, source, zz, i * self.part, self.part)
            self.out.send(
                view,
                view,
                self.send_sem.at[11 + 2 * k + i],
                self.half_sem.at[i, source * SIDE + zz],
                at(z, (y + step) % SIDE),
            )

    def open(self):
        z, y = self.z, self.y
        own = unit(self.buf, y, z)
        for k in (1, 2, 3):
            self.out.send(own, own, self.send_sem.at[k - 1], self.full_sem.at[y * SIDE + z], at(across(z, k), y))
        self.push(0)

    def steps(self):
        made = []
        for k in range(1, SIDE):
            made += [partial(self.push, k), partial(self.forward, k - 1)]
        return made + [partial(self.forward, SIDE - 1)]

    def run(self):
        self.open()
        for step in self.steps():
            step()

    def finish(self):
        z, y = self.z, self.y
        far = (y + 2) % SIDE
        for k in range(SIDE):
            zz = across(z, k)
            for i in range(2):
                view = unit(self.buf, far, zz, i * self.part, self.part)
                arrived(view, self.send_sem.at[0], self.half_sem.at[i, far * SIDE + zz], at(z, (y + 1) % SIDE))


def swapped(index, bit):
    step = 1 << bit
    return index + step - 2 * step * ((index // step) % 2)


def expert_kernel(
    bit,
    raw,
    scale_up,
    scale_down,
    tokens,
    routes,
    weights,
    up_hbm,
    down_hbm,
    up_out,
    down_out,
    slots,
    errors,
    up,
    down,
    pre,
    hidden,
    part,
    got_half,
    got_full,
    got_z,
    total,
    stage_out,
    stage_in,
    share_col,
    slope_in,
    up_mate,
    down_mate,
    load_sem,
    store_sem,
    stage_sem,
    gather_send,
    gather_full,
    gather_half,
    sum_send,
    sum_half,
    sum_full,
    sum_z,
    mate_send,
    mate_got,
    hidden_t,
    *more,
):
    z, y = place()
    half = tokens.shape[1] // 2
    quarter = half // 2
    units = up.shape[1]
    tile = min(TILE, half // 3)
    early = half // tile // 3
    out = Sender()
    y_up, y_down, y_far = (y + 1) % SIDE, (y + SIDE - 1) % SIDE, (y + 2) % SIDE
    y_pair = y + 1 - 2 * (y % 2)
    mate = {"island": swapped(lax.axis_index("island"), bit)}

    loads = [
        pltpu.make_async_copy(up_hbm, up, load_sem.at[0]),
        pltpu.make_async_copy(down_hbm, down, load_sem.at[1]),
    ]
    for load in loads:
        load.start()
    barrier = pltpu.get_barrier_semaphore()
    peers = [at(across(z, k), y) for k in (1, 2, 3)] + [at(z, y_up), at(z, y_down), mate]
    for peer in peers:
        pl.semaphore_signal(barrier, inc=1, device_id=peer, device_id_type=MESH)

    target0 = routes[0:1, :] == 0
    target1 = routes[1:2, :] == 0
    chosen = (target0 | target1).astype(F32)
    share_row = jnp.where(target0, weights[0:1, :], 0.0) + jnp.where(target1, weights[1:2, :], 0.0)
    count = chosen.shape[1]
    earlier = lax.broadcasted_iota(jnp.int32, (count, count), 0) <= lax.broadcasted_iota(jnp.int32, (count, count), 1)
    ranks = jnp.dot(
        jnp.broadcast_to(chosen, (8, count)).astype(BF16), earlier.astype(BF16), preferred_element_type=F32
    )[0:1, :]
    slot_ids = lax.broadcasted_iota(jnp.int32, (STAGE, count), 0).astype(F32)
    takes = (slot_ids == ranks - 1.0) & (chosen > 0.0) & (slot_ids < float(CAP))
    table = jnp.where(takes, 1.0, 0.0).astype(BF16)
    own_share = jnp.sum(jnp.where(takes, share_row, 0.0), axis=1, keepdims=True)
    mine = y % 2
    own_rows = jnp.dot(
        table, tokens[:, pl.ds(pl.multiple_of(mine * half, LANES), half)], preferred_element_type=F32
    )
    stage_out[:, 0:half] = jnp.dot(
        table, tokens[:, pl.ds(pl.multiple_of((1 - mine) * half, LANES), half)], preferred_element_type=F32
    ).astype(BF16)
    stage_out[:, half:] = jnp.broadcast_to(own_share, (STAGE, LANES)).astype(BF16)
    pl.semaphore_wait(barrier, len(peers))
    out.send(stage_out, stage_in, stage_sem.at[0], stage_sem.at[1], at(z, y_pair))
    arrived(stage_in, stage_sem.at[0], stage_sem.at[1], at(z, y_pair))
    other_rows = stage_in[:, 0:half].astype(F32)
    other_share = stage_in[:, half:].astype(F32)[0:CAP, 0:1]
    first = mine == 0
    own_rows, own_share, other_rows = own_rows[0:CAP], own_share[0:CAP], other_rows[0:CAP]
    rows = jnp.concatenate(
        [jnp.where(first, own_rows, other_rows), jnp.where(first, other_rows, own_rows)], axis=0
    ).astype(BF16)
    unit(slots, y, z)[...] = rows
    share_col[...] = jnp.broadcast_to(
        jnp.concatenate(
            [jnp.where(first, own_share, other_share), jnp.where(first, other_share, own_share)], axis=0
        ),
        (PAIR, LANES),
    )

    def gather(buf, i):
        return Gather(buf, gather_send.at[i], gather_full.at[i], gather_half.at[i], out)

    def tiles(ref, mat, i):
        begin = pl.ds(pl.multiple_of(i * tile, LANES), tile)
        return ref.at[begin, :] if mat == 0 else ref.at[:, begin]

    def tile_copy(src, mat, i):
        return pltpu.make_async_remote_copy(
            src_ref=tiles(src, mat, i),
            dst_ref=tiles((up_mate, down_mate)[mat], mat, i),
            send_sem=mate_send.at[mat, i],
            recv_sem=mate_got.at[mat, i],
            device_id=mate,
            device_id_type=MESH,
        )

    def send_tile(src, mat, i):
        tile_copy(src, mat, i).start()

    def wait_tile(mat, i):
        tile_copy((up_mate, down_mate)[mat], mat, i).wait_recv()

    spread = gather(slots, 0)
    if raw:
        slots_mate, errors_mate, hidden_mate, pre_mate, unit_send, unit_got = more
        spread_mate, back_mate = gather(slots_mate, 2), gather(errors_mate, 3)
        own_unit = unit(slots, y, z)
        out.send(own_unit, unit(slots_mate, y, z), unit_send.at[0], unit_got.at[0], mate)
        for i in range(2 * half // tile):
            send_tile(up_hbm, 0, i)
        for i in range(early):
            send_tile(down_hbm, 1, i)
    spread.run()
    if raw:
        arrived(unit(slots_mate, y, z), unit_send.at[0], unit_got.at[0], mate)
        spread_mate.open()

    def group_rows(group):
        return pl.ds(pl.multiple_of(group * GROUP, 16), GROUP)

    def lanes(i, size):
        return pl.ds(pl.multiple_of(i * size, LANES), size)

    def contract(block, left, right, right_t, finish):
        def step(n, carry):
            cols = lanes(n, UNIT_TILE)
            if right_t:
                first, second = right[cols, 0:half], right[cols, half:]
                dims = (((1,), (1,)), ((), ()))
            else:
                first, second = right[0:half, cols], right[half:, cols]
                dims = (((1,), (0,)), ((), ()))
            finish(
                cols,
                lax.dot_general(left[0, block, :], first, dims, preferred_element_type=F32)
                + lax.dot_general(left[1, block, :], second, dims, preferred_element_type=F32),
            )
            return carry

        lax.fori_loop(0, units // UNIT_TILE, step, 0)

    def ahead(group, slots, up, pre, hidden):
        block = group_rows(group)

        def finish(cols, values):
            values = scale_up * values
            pre[block, cols] = values
            hidden[block, cols] = jax.nn.silu(values).astype(BF16)

        contract(block, slots, up, False, finish)

    def column(yy):
        block = group_rows(yy // 2)
        side = yy % 2

        def step(j, carry):
            part[side, block, lanes(j, tile)] = (
                scale_down
                * jnp.dot(
                    hidden[block, :],
                    down[:, lanes(side * (half // tile) + j, tile)],
                    preferred_element_type=F32,
                )
            ).astype(BF16)
            return carry

        lax.fori_loop(0, half // tile, step, 0)

    def to(side):
        return (y + SIDE - 1 + 2 * side) % SIDE

    def send_rest(side):
        for k in (3, 2, 1, 0):
            zz = across(z, k)
            low = pl.multiple_of((1 - side) * quarter, LANES)
            out.send(
                unit(part, to(side), zz, low, quarter),
                got_full.at[side, zz, :, pl.ds(low, quarter)],
                sum_send.at[16 + 2 * k + side],
                sum_full.at[side, zz, 1],
                at(z, to(side)),
            )

    def send_far():
        for k in (3, 2, 1, 0):
            zz = across(z, k)
            for side in range(2):
                out.send(
                    unit(part, y_far, zz, side * quarter, quarter),
                    got_half.at[side, zz],
                    sum_send.at[2 * k + side],
                    sum_half.at[side, zz],
                    at(z, to(side)),
                )

    def add_far(k):
        zz = across(z, k)
        for side in range(2):
            low = side * quarter
            arrived(got_half.at[side, zz], sum_send.at[0], sum_half.at[side, zz], at(z, to(side)))
            view = unit(part, to(side), zz, low, quarter)
            view[...] = (view[...].astype(F32) + got_half[side, zz].astype(F32)).astype(BF16)
            out.send(
                view,
                got_full.at[side, zz, :, pl.ds(low, quarter)],
                sum_send.at[8 + 2 * k + side],
                sum_full.at[side, zz, 0],
                at(z, to(side)),
            )

    def collect(k):
        zz = across(z, k)
        for side in range(2):
            for low, sem in ((side * quarter, 0), ((1 - side) * quarter, 1)):
                arrived(
                    got_full.at[side, zz, :, pl.ds(low, quarter)], sum_send.at[0], sum_full.at[side, zz, sem], at(z, y_up)
                )
        view = unit(part, y, zz)
        added = view[...].astype(F32) + got_full[0, zz].astype(F32) + got_full[1, zz].astype(F32)
        if k == 0:
            total[...] = added
        else:
            view[...] = added.astype(BF16)
            out.send(view, got_z.at[k - 1], sum_send.at[23 + k], sum_z.at[k - 1], at(zz, y))

    for load in loads:
        load.wait()
    pair_side = 1 - y % 2
    ahead(y // 2, slots, up, pre, hidden)
    column(y_pair)
    send_rest(pair_side)
    spread.finish()
    ahead(1 - y // 2, slots, up, pre, hidden)
    column(y_far)
    send_far()
    column(to(1 - pair_side))
    send_rest(1 - pair_side)
    column(y)
    aside = spread_mate.steps() if raw else []
    add_far(3)
    add_far(2)
    collect(3)
    add_far(1)
    collect(2)
    add_far(0)
    for step in aside[:2]:
        step()
    collect(1)
    for step in aside[2:4]:
        step()
    collect(0)
    for step in aside[4:]:
        step()
    for k in (1, 2, 3):
        arrived(got_z.at[k - 1], sum_send.at[0], sum_z.at[k - 1], at(across(z, k), y))
    result = total[...] + got_z[0].astype(F32) + got_z[1].astype(F32) + got_z[2].astype(F32)
    share = share_col[:, 0:1]
    unit(errors, y, z)[...] = (share * (share * result - unit(slots, y, z)[...].astype(F32))).astype(BF16)

    back = gather(errors, 1)
    if raw:
        own_unit = unit(errors, y, z)
        out.send(own_unit, unit(errors_mate, y, z), unit_send.at[1], unit_got.at[1], mate)
        for i in range(early, 2 * half // tile):
            send_tile(down_hbm, 1, i)
    back.run()

    def slopes(group, errors, down, pre, slope_in):
        block = group_rows(group)

        def finish(cols, values):
            slope_in[block, cols] = (scale_down * values * silu_slope(pre[block, cols])).astype(BF16)

        contract(block, errors, down, True, finish)

    def turn(hidden):
        def step(j, carry):
            rows = pl.ds(pl.multiple_of(j * LANES, 16), LANES)
            hidden_t[:, lanes(j, LANES)] = hidden[rows, :].T
            return carry

        lax.fori_loop(0, hidden.shape[0] // LANES, step, 0)

    over_slots = (((0,), (0,)), ((), ()))

    def moved(mat, i, slots, errors, up, down, slope_in):
        side, cols = i // (half // tile), lanes(i % (half // tile), tile)
        if mat == 0:
            change = scale_up * lax.dot_general(
                slots[side, :, cols], slope_in[...], over_slots, preferred_element_type=F32
            )
            old = tiles(up, 0, i)[...]
        else:
            change = scale_down * jnp.dot(hidden_t[...], errors[side, :, cols], preferred_element_type=F32)
            old = tiles(down, 1, i)[...]
        return (old.astype(F32) - learn_rate * change).astype(BF16)

    own = (slots, errors, up, down, slope_in)
    count = 2 * half // tile

    def every_tile(body, first=0, last=None):
        def step(i, carry):
            for mat in (1, 0):
                body(mat, i)
            return carry

        lax.fori_loop(first, count if last is None else last, step, 0)

    def own_tile(mat, i):
        tiles((up, down)[mat], mat, i)[...] = moved(mat, i, *own)

    def store_of(mat, i):
        ref = (up_mate, down_mate)[mat]
        return pltpu.make_async_copy(
            tiles(ref, mat, i), tiles((up_out, down_out)[mat], mat, i), store_sem.at[mat, i]
        )

    def blend(mat, i, theirs):
        mine = tiles((up, down)[mat], mat, i)[...]
        tiles((up_mate, down_mate)[mat], mat, i)[...] = (
            0.5 * (mine.astype(F32) + theirs.astype(F32))
        ).astype(BF16)
        store_of(mat, i).start()

    if raw:
        arrived(unit(errors_mate, y, z), unit_send.at[1], unit_got.at[1], mate)
        back_mate.open()
        steps = back_mate.steps()
        slopes(y // 2, errors, down, pre, slope_in)
        steps[0]()
        back.finish()
        slopes(1 - y // 2, errors, down, pre, slope_in)
        steps[1]()
        turn(hidden)
        for n in range(4):
            steps[2 + n]()
            every_tile(own_tile, n * count // 4, (n + 1) * count // 4)
        steps[6]()
        spread_mate.finish()

        def wait_up(i, carry):
            wait_tile(0, i)
            return carry

        def wait_down(i, carry):
            wait_tile(1, i)
            return carry

        lax.fori_loop(0, count, wait_up, 0)
        for group in range(2):
            ahead(group, slots_mate, up_mate, pre_mate, hidden_mate)
        turn(hidden_mate)
        lax.fori_loop(0, count, wait_down, 0)
        slopes(y // 2, errors_mate, down_mate, pre_mate, slope_in)
        back_mate.finish()
        slopes(1 - y // 2, errors_mate, down_mate, pre_mate, slope_in)
        theirs = (slots_mate, errors_mate, up_mate, down_mate, slope_in)
        every_tile(lambda mat, i: blend(mat, i, moved(mat, i, *theirs)))
    else:
        turn(hidden)
        slopes(y // 2, errors, down, pre, slope_in)
        back.finish()
        slopes(1 - y // 2, errors, down, pre, slope_in)

        def move_and_send(mat, i):
            own_tile(mat, i)
            send_tile((up, down)[mat], mat, i)

        def meet(mat, i):
            wait_tile(mat, i)
            blend(mat, i, tiles((up_mate, down_mate)[mat], mat, i)[...])

        every_tile(move_and_send)
        every_tile(meet)

    def settle(mat, i):
        tile_copy((up_hbm, down_hbm)[mat] if raw else (up, down)[mat], mat, i).wait_send()
        store_of(mat, i).wait()

    every_tile(settle)
    out.drain()


def expert(bit, raw, tokens, routes, weights, up, down):
    width = tokens.shape[1]
    units = up.shape[1]
    half = width // 2
    tiles = width // min(TILE, half // 3)
    slot_count = SIDE * SIDE * CAP
    hidden_total = units * SIDE * SIDE
    vmem = pl.BlockSpec(memory_space=pltpu.VMEM)
    hbm = pl.BlockSpec(memory_space=pl.ANY)
    dma = pltpu.SemaphoreType.DMA
    all_rows = pltpu.VMEM((2, slot_count, half), BF16)
    gathers = 4 if raw else 2
    more = []
    if raw:
        more = [
            all_rows,
            all_rows,
            pltpu.VMEM((slot_count, units), BF16),
            pltpu.VMEM((slot_count, units), F32),
            dma((2,)),
            dma((2,)),
        ]
    return pl.pallas_call(
        partial(expert_kernel, bit, raw, width ** (-0.5), hidden_total ** (-0.5)),
        out_shape=(
            jax.ShapeDtypeStruct((width, units), BF16),
            jax.ShapeDtypeStruct((units, width), BF16),
        ),
        in_specs=[vmem, vmem, vmem, hbm, hbm],
        out_specs=(hbm, hbm),
        scratch_shapes=[
            all_rows,
            all_rows,
            pltpu.VMEM((width, units), BF16),
            pltpu.VMEM((units, width), BF16),
            pltpu.VMEM((slot_count, units), F32),
            pltpu.VMEM((slot_count, units), BF16),
            all_rows,
            pltpu.VMEM((2, SIDE, PAIR, half // 2), BF16),
            pltpu.VMEM((2, SIDE, PAIR, half), BF16),
            pltpu.VMEM((SIDE - 1, PAIR, half), BF16),
            pltpu.VMEM((PAIR, half), F32),
            pltpu.VMEM((STAGE, half + LANES), BF16),
            pltpu.VMEM((STAGE, half + LANES), BF16),
            pltpu.VMEM((PAIR, LANES), F32),
            pltpu.VMEM((slot_count, units), BF16),
            pltpu.VMEM((width, units), BF16),
            pltpu.VMEM((units, width), BF16),
            dma((2,)),
            dma((2, tiles)),
            dma((2,)),
            dma((gathers, 19)),
            dma((gathers, SIDE * SIDE)),
            dma((gathers, 2, SIDE * SIDE)),
            dma((27,)),
            dma((2, SIDE)),
            dma((2, SIDE, 2)),
            dma((SIDE - 1,)),
            dma((2, tiles)),
            dma((2, tiles)),
            pltpu.VMEM((units, slot_count), BF16),
        ]
        + more,
        compiler_params=pltpu.CompilerParams(
            collective_id=bit, has_side_effects=True, vmem_limit_bytes=60 * 1024 * 1024
        ),
        cost_estimate=pl.CostEstimate(
            flops=10 * slot_count * width * units, bytes_accessed=200_000_000, transcendentals=2 * slot_count * units
        ),
    )(tokens, routes, weights, up, down)


RAW_BITS = (1, 2)


def on_device(tokens, routing, router_weight, w_up, w_down, step_number):
    levels = lax.axis_size("island").bit_length() - 1
    bit_index = jnp.remainder(step_number[0], jnp.int32(levels))
    new_up, new_down = lax.switch(
        bit_index,
        [partial(expert, bit, bit in RAW_BITS) for bit in range(levels)],
        tokens[0],
        routing[0].T,
        router_weight[0].T.astype(F32),
        w_up[0],
        w_down[0],
    )
    return (new_up[None], new_down[None])


def solution(mesh):
    placed = (
        P("island", "fsdp", None),
        P("island", "fsdp", None),
        P("island", "fsdp", None),
        P("island", None, "fsdp"),
        P("island", "fsdp", None),
        P(),
    )
    return jax.shard_map(
        on_device,
        mesh=mesh,
        in_specs=placed,
        out_specs=(P("island", None, "fsdp"), P("island", "fsdp", None)),
        check_vma=False,
    )
```

time: 313 us -> 406 us (1.30)
  the two profiles are of different devices: /device:TPU:228 before, /device:TPU:64 now
where the time goes in v2:
time: 406 us
  Pallas kernels  399 us (98%)
  local copies, waits for them, and re-layouts  4.68 us (1%)
    pallas_call x1, Pallas kernels, expert(): pl.pallas_call(partial(expert_kernel, bit, raw, width ** (-0.5), hidden_t...  399 us

profile of v2, /device:TPU:64, one launch (start us, length us, event | category | flops | bytes accessed | tf_op | source)
XLA Modules:
  0.0 406.0 jit_solution(15880281761257916387)
XLA Ops:
  1.3 0.7 convert_bitcast_fusion
  2.0 399.3 %conditional.1 = ((bf16[3072,512]{1,0:T(8,128)(2,1)S(1)}, bf16[512,3072]{1,0:T(8,128)(2,1)})) conditional(s32[]{:T(128)} %clamp.3, (bf16[1,128,3072]{2,1,0:T(8,128)(2,1)}, bf16[1,3072,512]{2,1,0:T(8,128)(2,1)}, bf16[1,512,3072]{2,1,0:T(8,128)(2,1)}, s32[2,128]{1,0:T(2,128)}, f32[2,128]{1,0:T(2,128)S(1)}) %tuple.47, ...), branch_computations={%region_0.1_spmd, %region_1.2_spmd, %region_2.3_spmd, %region_3.4_... | conditional | flops 10066329600 | bytes 200000000 | solution.py:632
  2.0 399.0 %branch_3_fun.1 = (bf16[3072,512]{1,0:T(8,128)(2,1)S(1)}, bf16[512,3072]{1,0:T(8,128)(2,1)}) custom-call(bf16[128,3072]{1,0:T(8,128)(2,1)} %bitcast.39, s32[2,128]{1,0:T(2,128)} %get-tuple-element.84.routes, f32[2,128]{1,0:T(2,128)S(1)} %get-tuple-element.85.weights, bf16[3072,512]{1,0:T(8,128)(2,1)} %bitcast.31, bf16[512,3072]{1,0:T(8,128)(2,1)} %bitcast.35), custom_call_target="tpu_custom_call" | custom-call | flops 10066329600 | bytes 200000000 | tf_op jit(solution)/shard_map/cond/branch_3_fun/pallas_call | solution.py:576
  401.3 0.0 copy-start
  401.3 1.7 copy.19
  402.9 1.3 copy-done
  404.3 1.7 copy.20
Async XLA Ops:
  401.3 3.0 copy-start

commit v3 on v2

--- a/solution.py
+++ b/solution.py
@@ -77,7 +77,7 @@
     def __init__(self, buf, send_sem, full_sem, half_sem, out):
         self.buf, self.send_sem, self.full_sem, self.half_sem, self.out = buf, send_sem, full_sem, half_sem, out
         self.z, self.y = place()
-        self.part = buf.shape[-1] // 2
+        self.width = buf.shape[-1]
 
     def wait_full(self, yy, zz):
         view = unit(self.buf, yy, zz)
@@ -94,13 +94,20 @@
                 view, view, self.send_sem.at[3 + 2 * k + i], self.full_sem.at[y * SIDE + zz], at(z, (y + step) % SIDE)
             )
 
+    def side(self, k, i):
+        size = self.width // (2 if k == 0 else 3)
+        return i * (self.width - size), size
+
+    def middle(self, zz):
+        return unit(self.buf, (self.y + 2) % SIDE, zz, self.width // 3, self.width // 3)
+
     def forward(self, k):
         z, y = self.z, self.y
         zz = across(z, k)
         for i, step in enumerate((1, SIDE - 1)):
             source = (y + SIDE - step) % SIDE
             self.wait_full(source, zz)
-            view = unit(self.buf, source, zz, i * self.part, self.part)
+            view = unit(self.buf, source, zz, *self.side(k, i))
             self.out.send(
                 view,
                 view,
@@ -120,21 +127,33 @@
         made = []
         for k in range(1, SIDE):
             made += [partial(self.push, k), partial(self.forward, k - 1)]
-        return made + [partial(self.forward, SIDE - 1)]
+        return made + [self.share_far, partial(self.forward, SIDE - 1)]
 
     def run(self):
         self.open()
         for step in self.steps():
             step()
 
+    def wait_far(self, k):
+        z, y = self.z, self.y
+        far, zz = (y + 2) % SIDE, across(z, k)
+        for i in range(2):
+            view = unit(self.buf, far, zz, *self.side(k, i))
+            arrived(view, self.send_sem.at[0], self.half_sem.at[i, far * SIDE + zz], at(z, (y + 1) % SIDE))
+
+    def share_far(self):
+        z, y = self.z, self.y
+        self.wait_far(0)
+        view = self.middle(z)
+        for k in (1, 2, 3):
+            self.out.send(view, view, self.send_sem.at[18 + k], self.half_sem.at[2, z], at(across(z, k), y))
+
     def finish(self):
-        z, y = self.z, self.y
-        far = (y + 2) % SIDE
-        for k in range(SIDE):
-            zz = across(z, k)
-            for i in range(2):
-                view = unit(self.buf, far, zz, i * self.part, self.part)
-                arrived(view, self.send_sem.at[0], self.half_sem.at[i, far * SIDE + zz], at(z, (y + 1) % SIDE))
+        for k in (1, 2, 3):
+            self.wait_far(k)
+        for k in (1, 2, 3):
+            zz = across(self.z, k)
+            arrived(self.middle(zz), self.send_sem.at[0], self.half_sem.at[2, zz], at(zz, self.y))
 
 
 def swapped(index, bit):
@@ -184,18 +203,40 @@
     mate_send,
     mate_got,
     hidden_t,
+    slots_t,
+    got_third,
+    third_got,
     *more,
 ):
     z, y = place()
     half = tokens.shape[1] // 2
-    quarter = half // 2
     units = up.shape[1]
     tile = min(TILE, half // 3)
-    early = half // tile // 3
+    early = max(2 * half // tile // 3, 1)
     out = Sender()
     y_up, y_down, y_far = (y + 1) % SIDE, (y + SIDE - 1) % SIDE, (y + 2) % SIDE
     y_pair = y + 1 - 2 * (y % 2)
     mate = {"island": swapped(lax.axis_index("island"), bit)}
+
+    def tiles(ref, mat, i):
+        begin = pl.ds(pl.multiple_of(i * tile, LANES), tile)
+        return ref.at[begin, :] if mat == 0 else ref.at[:, begin]
+
+    def tile_copy(src, mat, i):
+        return pltpu.make_async_remote_copy(
+            src_ref=tiles(src, mat, i),
+            dst_ref=tiles((up_mate, down_mate)[mat], mat, i),
+            send_sem=mate_send.at[mat, i],
+            recv_sem=mate_got.at[mat, i],
+            device_id=mate,
+            device_id_type=MESH,
+        )
+
+    def send_tile(src, mat, i):
+        tile_copy(src, mat, i).start()
+
+    def wait_tile(mat, i):
+        tile_copy((up_mate, down_mate)[mat], mat, i).wait_recv()
 
     loads = [
         pltpu.make_async_copy(up_hbm, up, load_sem.at[0]),
@@ -211,7 +252,8 @@
     target0 = routes[0:1, :] == 0
     target1 = routes[1:2, :] == 0
     chosen = (target0 | target1).astype(F32)
-    share_row = jnp.where(target0, weights[0:1, :], 0.0) + jnp.where(target1, weights[1:2, :], 0.0)
+    weight = weights[...].astype(F32)
+    share_row = jnp.where(target0, weight[0:1, :], 0.0) + jnp.where(target1, weight[1:2, :], 0.0)
     count = chosen.shape[1]
     earlier = lax.broadcasted_iota(jnp.int32, (count, count), 0) <= lax.broadcasted_iota(jnp.int32, (count, count), 1)
     ranks = jnp.dot(
@@ -231,6 +273,9 @@
     stage_out[:, half:] = jnp.broadcast_to(own_share, (STAGE, LANES)).astype(BF16)
     pl.semaphore_wait(barrier, len(peers))
     out.send(stage_out, stage_in, stage_sem.at[0], stage_sem.at[1], at(z, y_pair))
+    if raw:
+        for i in range(early):
+            send_tile(up_hbm, 0, i)
     arrived(stage_in, stage_sem.at[0], stage_sem.at[1], at(z, y_pair))
     other_rows = stage_in[:, 0:half].astype(F32)
     other_share = stage_in[:, half:].astype(F32)[0:CAP, 0:1]
@@ -250,33 +295,13 @@
     def gather(buf, i):
         return Gather(buf, gather_send.at[i], gather_full.at[i], gather_half.at[i], out)
 
-    def tiles(ref, mat, i):
-        begin = pl.ds(pl.multiple_of(i * tile, LANES), tile)
-        return ref.at[begin, :] if mat == 0 else ref.at[:, begin]
-
-    def tile_copy(src, mat, i):
-        return pltpu.make_async_remote_copy(
-            src_ref=tiles(src, mat, i),
-            dst_ref=tiles((up_mate, down_mate)[mat], mat, i),
-            send_sem=mate_send.at[mat, i],
-            recv_sem=mate_got.at[mat, i],
-            device_id=mate,
-            device_id_type=MESH,
-        )
-
-    def send_tile(src, mat, i):
-        tile_copy(src, mat, i).start()
-
-    def wait_tile(mat, i):
-        tile_copy((up_mate, down_mate)[mat], mat, i).wait_recv()
-
     spread = gather(slots, 0)
     if raw:
         slots_mate, errors_mate, hidden_mate, pre_mate, unit_send, unit_got = more
         spread_mate, back_mate = gather(slots_mate, 2), gather(errors_mate, 3)
         own_unit = unit(slots, y, z)
         out.send(own_unit, unit(slots_mate, y, z), unit_send.at[0], unit_got.at[0], mate)
-        for i in range(2 * half // tile):
+        for i in range(early, 2 * half // tile):
             send_tile(up_hbm, 0, i)
         for i in range(early):
             send_tile(down_hbm, 1, i)
@@ -339,40 +364,68 @@
     def to(side):
         return (y + SIDE - 1 + 2 * side) % SIDE
 
+    def size_of(k):
+        return half // (2 if k == 0 else 3)
+
+    def far_cols(k, side):
+        return side * (half - size_of(k)), size_of(k)
+
+    def rest_cols(k, side):
+        return pl.multiple_of((1 - side) * size_of(k), LANES), half - size_of(k)
+
     def send_rest(side):
         for k in (3, 2, 1, 0):
             zz = across(z, k)
-            low = pl.multiple_of((1 - side) * quarter, LANES)
+            low, size = rest_cols(k, side)
             out.send(
-                unit(part, to(side), zz, low, quarter),
-                got_full.at[side, zz, :, pl.ds(low, quarter)],
+                unit(part, to(side), zz, low, size),
+                got_full.at[side, zz, :, pl.ds(low, size)],
                 sum_send.at[16 + 2 * k + side],
                 sum_full.at[side, zz, 1],
                 at(z, to(side)),
             )
 
-    def send_far():
-        for k in (3, 2, 1, 0):
-            zz = across(z, k)
-            for side in range(2):
-                out.send(
-                    unit(part, y_far, zz, side * quarter, quarter),
-                    got_half.at[side, zz],
-                    sum_send.at[2 * k + side],
-                    sum_half.at[side, zz],
-                    at(z, to(side)),
-                )
+    def send_middle():
+        for k in (1, 2, 3):
+            out.send(
+                unit(part, y_far, across(z, k), half // 3, half // 3),
+                got_third.at[k - 1],
+                sum_send.at[26 + k],
+                third_got.at[k - 1],
+                at(across(z, k), y),
+            )
+
+    def add_middle():
+        for k in (1, 2, 3):
+            arrived(got_third.at[k - 1], sum_send.at[0], third_got.at[k - 1], at(across(z, k), y))
+        view = unit(part, y_far, z, half // 3, half // 3)
+        view[...] = (
+            view[...].astype(F32) + got_third[0].astype(F32) + got_third[1].astype(F32) + got_third[2].astype(F32)
+        ).astype(BF16)
+
+    def send_far(k):
+        zz = across(z, k)
+        for side in range(2):
+            low, size = far_cols(k, side)
+            out.send(
+                unit(part, y_far, zz, low, size),
+                got_half.at[side, zz, :, pl.ds(0, size)],
+                sum_send.at[2 * k + side],
+                sum_half.at[side, zz],
+                at(z, to(side)),
+            )
 
     def add_far(k):
         zz = across(z, k)
         for side in range(2):
-            low = side * quarter
-            arrived(got_half.at[side, zz], sum_send.at[0], sum_half.at[side, zz], at(z, to(side)))
-            view = unit(part, to(side), zz, low, quarter)
-            view[...] = (view[...].astype(F32) + got_half[side, zz].astype(F32)).astype(BF16)
+            low, size = far_cols(k, side)
+            got = got_half.at[side, zz, :, pl.ds(0, size)]
+            arrived(got, sum_send.at[0], sum_half.at[side, zz], at(z, to(side)))
+            view = unit(part, to(side), zz, low, size)
+            view[...] = (view[...].astype(F32) + got[...].astype(F32)).astype(BF16)
             out.send(
                 view,
-                got_full.at[side, zz, :, pl.ds(low, quarter)],
+                got_full.at[side, zz, :, pl.ds(low, size)],
                 sum_send.at[8 + 2 * k + side],
                 sum_full.at[side, zz, 0],
                 at(z, to(side)),
@@ -381,9 +434,9 @@
     def collect(k):
         zz = across(z, k)
         for side in range(2):
-            for low, sem in ((side * quarter, 0), ((1 - side) * quarter, 1)):
+            for sem, (low, size) in enumerate((far_cols(k, side), rest_cols(k, side))):
                 arrived(
-                    got_full.at[side, zz, :, pl.ds(low, quarter)], sum_send.at[0], sum_full.at[side, zz, sem], at(z, y_up)
+                    got_full.at[side, zz, :, pl.ds(low, size)], sum_send.at[0], sum_full.at[side, zz, sem], at(z, y_up)
                 )
         view = unit(part, y, zz)
         added = view[...].astype(F32) + got_full[0, zz].astype(F32) + got_full[1, zz].astype(F32)
@@ -402,10 +455,14 @@
     spread.finish()
     ahead(1 - y // 2, slots, up, pre, hidden)
     column(y_far)
-    send_far()
+    send_middle()
+    for k in (3, 2, 1):
+        send_far(k)
     column(to(1 - pair_side))
     send_rest(1 - pair_side)
     column(y)
+    add_middle()
+    send_far(0)
     aside = spread_mate.steps() if raw else []
     add_far(3)
     add_far(2)
@@ -443,29 +500,40 @@
 
         contract(block, errors, down, True, finish)
 
-    def turn(hidden):
+    def both(body):
+        def step(group, carry):
+            body(group)
+            return carry
+
+        lax.fori_loop(0, 2, step, 0)
+
+    def turn(hidden, slots):
         def step(j, carry):
             rows = pl.ds(pl.multiple_of(j * LANES, 16), LANES)
-            hidden_t[:, lanes(j, LANES)] = hidden[rows, :].T
+            hidden_t[rows, :] = hidden[:, lanes(j, LANES)].T
             return carry
 
-        lax.fori_loop(0, hidden.shape[0] // LANES, step, 0)
-
-    over_slots = (((0,), (0,)), ((), ()))
-
-    def moved(mat, i, slots, errors, up, down, slope_in):
-        side, cols = i // (half // tile), lanes(i % (half // tile), tile)
+        def step_slots(j, carry):
+            blocks = half // LANES
+            rows = pl.ds(pl.multiple_of(j * LANES, 16), LANES)
+            slots_t[rows, :] = slots[j // blocks, :, lanes(j % blocks, LANES)].T
+            return carry
+
+        lax.fori_loop(0, units // LANES, step, 0)
+        lax.fori_loop(0, 2 * half // LANES, step_slots, 0)
+
+    def moved(mat, i, errors, up, down, slope_in):
         if mat == 0:
-            change = scale_up * lax.dot_general(
-                slots[side, :, cols], slope_in[...], over_slots, preferred_element_type=F32
-            )
+            rows = pl.ds(pl.multiple_of(i * tile, LANES), tile)
+            change = scale_up * jnp.dot(slots_t[rows, :], slope_in[...], preferred_element_type=F32)
             old = tiles(up, 0, i)[...]
         else:
+            side, cols = i // (half // tile), lanes(i % (half // tile), tile)
             change = scale_down * jnp.dot(hidden_t[...], errors[side, :, cols], preferred_element_type=F32)
             old = tiles(down, 1, i)[...]
         return (old.astype(F32) - learn_rate * change).astype(BF16)
 
-    own = (slots, errors, up, down, slope_in)
+    own = (errors, up, down, slope_in)
     count = 2 * half // tile
 
     def every_tile(body, first=0, last=None):
@@ -496,16 +564,6 @@
         arrived(unit(errors_mate, y, z), unit_send.at[1], unit_got.at[1], mate)
         back_mate.open()
         steps = back_mate.steps()
-        slopes(y // 2, errors, down, pre, slope_in)
-        steps[0]()
-        back.finish()
-        slopes(1 - y // 2, errors, down, pre, slope_in)
-        steps[1]()
-        turn(hidden)
-        for n in range(4):
-            steps[2 + n]()
-            every_tile(own_tile, n * count // 4, (n + 1) * count // 4)
-        steps[6]()
         spread_mate.finish()
 
         def wait_up(i, carry):
@@ -517,20 +575,29 @@
             return carry
 
         lax.fori_loop(0, count, wait_up, 0)
-        for group in range(2):
-            ahead(group, slots_mate, up_mate, pre_mate, hidden_mate)
-        turn(hidden_mate)
+        for step in steps[:1]:
+            step()
+        both(lambda group: ahead(group, slots_mate, up_mate, pre_mate, hidden_mate))
+        for step in steps[1:3]:
+            step()
+        back.finish()
+        both(lambda group: slopes(group, errors, down, pre, slope_in))
+        for step in steps[3:5]:
+            step()
+        turn(hidden, slots)
+        every_tile(own_tile)
+        for step in steps[5:]:
+            step()
+        turn(hidden_mate, slots_mate)
         lax.fori_loop(0, count, wait_down, 0)
-        slopes(y // 2, errors_mate, down_mate, pre_mate, slope_in)
         back_mate.finish()
-        slopes(1 - y // 2, errors_mate, down_mate, pre_mate, slope_in)
-        theirs = (slots_mate, errors_mate, up_mate, down_mate, slope_in)
+        both(lambda group: slopes(group, errors_mate, down_mate, pre_mate, slope_in))
+        theirs = (errors_mate, up_mate, down_mate, slope_in)
         every_tile(lambda mat, i: blend(mat, i, moved(mat, i, *theirs)))
     else:
-        turn(hidden)
-        slopes(y // 2, errors, down, pre, slope_in)
+        turn(hidden, slots)
         back.finish()
-        slopes(1 - y // 2, errors, down, pre, slope_in)
+        both(lambda group: slopes(group, errors, down, pre, slope_in))
 
         def move_and_send(mat, i):
             own_tile(mat, i)
@@ -602,20 +669,23 @@
             dma((2,)),
             dma((2, tiles)),
             dma((2,)),
-            dma((gathers, 19)),
+            dma((gathers, 22)),
             dma((gathers, SIDE * SIDE)),
-            dma((gathers, 2, SIDE * SIDE)),
-            dma((27,)),
+            dma((gathers, 3, SIDE * SIDE)),
+            dma((30,)),
             dma((2, SIDE)),
             dma((2, SIDE, 2)),
             dma((SIDE - 1,)),
             dma((2, tiles)),
             dma((2, tiles)),
             pltpu.VMEM((units, slot_count), BF16),
+            pltpu.VMEM((width, slot_count), BF16),
+            pltpu.VMEM((SIDE - 1, PAIR, half // 3), BF16),
+            dma((SIDE - 1,)),
         ]
         + more,
         compiler_params=pltpu.CompilerParams(
-            collective_id=bit, has_side_effects=True, vmem_limit_bytes=60 * 1024 * 1024
+            collective_id=bit, has_side_effects=True, vmem_limit_bytes=56 * 1024 * 1024
         ),
         cost_estimate=pl.CostEstimate(
             flops=10 * slot_count * width * units, bytes_accessed=200_000_000, transcendentals=2 * slot_count * units
@@ -634,7 +704,7 @@
         [partial(expert, bit, bit in RAW_BITS) for bit in range(levels)],
         tokens[0],
         routing[0].T,
-        router_weight[0].T.astype(F32),
+        router_weight[0].T,
         w_up[0],
         w_down[0],
     )

time: 406 us -> 147 us (0.36)
  the two profiles are of different devices: /device:TPU:64 before, /device:TPU:2 now
where the time goes in v3:
time: 147 us; the launch traced here: 146 us
  Pallas kernels  140 us (95%)
  local copies, waits for them, and re-layouts  3.33 us (2%)
    pallas_call x1, Pallas kernels, expert(): pl.pallas_call(partial(expert_kernel, bit, raw, width ** (-0.5), hidden_t...  140 us
    unnamed x2, local copies, waits for them, and re-layouts  3.33 us

profile of v3, /device:TPU:2, one launch (start us, length us, event | category | flops | bytes accessed | tf_op | source)
XLA Modules:
  0.0 145.6 jit_solution(15969273847569208293)
XLA Ops:
  1.3 141.0 %conditional.1 = ((bf16[3072,512]{1,0:T(8,128)(2,1)S(1)}, bf16[512,3072]{1,0:T(8,128)(2,1)S(1)})) conditional(s32[]{:T(128)} %clamp.3, (bf16[1,128,3072]{2,1,0:T(8,128)(2,1)}, bf16[1,3072,512]{2,1,0:T(8,128)(2,1)}, bf16[1,512,3072]{2,1,0:T(8,128)(2,1)}, s32[2,128]{1,0:T(2,128)}, bf16[2,128]{1,0:T(2,128)(2,1)}) %tuple.51, ...), branch_computations={%region_0.1_spmd, %region_1.2_spmd, %region_2.3_spmd, %region_3.4_... | conditional | flops 10066329600 | bytes 200000000 | solution.py:702
  1.3 140.2 %branch_0_fun.1 = (bf16[3072,512]{1,0:T(8,128)(2,1)S(1)}, bf16[512,3072]{1,0:T(8,128)(2,1)S(1)}) custom-call(bf16[128,3072]{1,0:T(8,128)(2,1)} %bitcast.34, s32[2,128]{1,0:T(2,128)} %get-tuple-element.63.routes, bf16[2,128]{1,0:T(2,128)(2,1)} %get-tuple-element.64.weights, bf16[3072,512]{1,0:T(8,128)(2,1)} %bitcast.26, bf16[512,3072]{1,0:T(8,128)(2,1)} %bitcast.30), custom_call_target="tpu_custom_call" | custom-call | flops 10066329600 | bytes 200000000 | tf_op jit(solution)/shard_map/cond/branch_0_fun/pallas_call | solution.py:643
  142.3 1.7 %copy.19 = bf16[1,3072,512]{2,1,0:T(8,128)(2,1)} copy(bf16[1,3072,512]{2,1,0:T(8,128)(2,1)S(1)} %bitcast.24) | data formatting | bytes 6291456
  143.9 1.7 %copy.20 = bf16[1,512,3072]{2,1,0:T(8,128)(2,1)} copy(bf16[1,512,3072]{2,1,0:T(8,128)(2,1)S(1)} %bitcast.25) | data formatting | bytes 6291456
